TPU v7x, 32 devices: a whole 2x2x4 slice. The times are simulated.
32 devices in a mesh: role: 2 (over x), shard: 4 (over z), rep: 4 (over y, core).
Axes of the slice: x: 2, y: 2, z: 4, core: 2. Of those that a mesh axis runs over, the one named last changes fastest.
Arguments:
- qkv_versions: bfloat16 [2, 5120, 7168], P('role', 'rep', 'shard'), may hold values from -0.078125 to 0.078125
- qkv_bias: bfloat16 [2, 7168], P('role'), may hold values from -3 to 3
- o_versions: bfloat16 [2, 5120, 5120], P('role', 'rep', 'shard'), may hold values from -0.078125 to 0.078125
- norm_gain: bfloat16 [2, 5120], P('role'), may hold values from 0.5 to 1.5
- hidden: bfloat16 [2, 256, 4, 5120], P('role', ('shard', 'rep')), may hold values from -6 to 6
- cache_keys: bfloat16 [2, 256, 128, 1024], P('role', ('shard', 'rep')), may hold values from -220 to 220
- cache_values: bfloat16 [2, 256, 128, 1024], P('role', ('shard', 'rep')), may hold values from -6 to 6
- lengths: int32 [2, 256], P('role', ('shard', 'rep')), may hold values from 2 to 128, as said below
Outputs:
- layer_out: bfloat16 [2, 256, 4, 5120], P('role', ('shard', 'rep'))
- new_qkv: bfloat16 [2, 5120, 7168], P('role', 'rep', 'shard')
- new_o: bfloat16 [2, 5120, 5120], P('role', 'rep', 'shard')
Inputs may be any that keep to these rules, and one draw needn't show every extreme that they name: `lengths`: in every aligned group of 16 rows of a role at least one row has all 128 positions live.
All inputs are finite; a program needn't handle non-finite values.
Results may differ from a plain program's by a relative error of at most 0.0065.
The roundings to bfloat16 on the way count: a program that leaves them out, or rounds other values in their place, can miss the bound.
Values may be sent and summed in bfloat16 or wider, within the bound.
A program may use at most 128 MiB of HBM per device.

v0:
```python
import math

import jax
import jax.numpy as jnp
from jax import lax
from jax.sharding import PartitionSpec as P

FACTOR_A = 40
FACTOR_B = 128
D = 5120
HEADS = 40
KV_HEADS = 8
HEAD_DIM = 128
QDIM = 5120
KVD = 1024
STEPS = 4


EPSILON = 1e-06
ROPE_BASE = 1000000.0


def shifted(value, axis, steps):
    count = lax.axis_size(axis)
    initial, last = (max(0, -steps), min(count, count - steps))
    return lax.ppermute(value, axis, [(source, source + steps) for source in range(initial, last)])


def hadamard_pair():
    modulus = FACTOR_A // 2 - 1
    residues = jnp.arange(modulus, dtype=jnp.int32)
    squares = jnp.arange(1, modulus, dtype=jnp.int32) ** 2 % modulus
    differ = (residues[None, :] - residues[:, None]) % modulus
    residue_mask = jnp.any(differ[:, :, None] == squares[None, None, :], axis=2)
    jacobs = jnp.where(differ == 0, 0.0, jnp.where(residue_mask, 1.0, -1.0)).astype(jnp.float32)
    top_row = jnp.concatenate(
        [jnp.zeros((1, 1), jnp.float32), jnp.ones((1, modulus), jnp.float32)], axis=1
    )
    lower_rows = jnp.concatenate([-jnp.ones((modulus, 1), jnp.float32), jacobs], axis=1)
    paley_core = jnp.eye(modulus + 1, dtype=jnp.float32) + jnp.concatenate(
        [top_row, lower_rows], axis=0
    )
    doubler = jnp.array([[1.0, 1.0], [1.0, -1.0]], jnp.float32)
    outer_factor = jnp.kron(doubler, paley_core)
    indices = jnp.arange(FACTOR_B, dtype=jnp.int32)
    common_bits = indices[:, None] & indices[None, :]
    parity = jnp.zeros((FACTOR_B, FACTOR_B), jnp.int32)
    for bit_level in range(FACTOR_B.bit_length() - 1):
        parity = parity + (common_bits >> bit_level & 1)
    inner_factor = (1 - 2 * (parity % 2)).astype(jnp.float32)
    return (outer_factor, inner_factor)


def rotate_row_part(full_rows, part_index, part_total):
    outer_factor, inner_factor = hadamard_pair()
    blocks = full_rows.reshape(FACTOR_A, FACTOR_B, full_rows.shape[1])
    inner_mixed = jnp.einsum(
        "abc,by->ayc", blocks, inner_factor.astype(jnp.bfloat16), preferred_element_type=jnp.float32
    )
    part_width = FACTOR_A // part_total
    outer_part = lax.dynamic_slice_in_dim(outer_factor, part_index * part_width, part_width, 1)
    turned = jnp.einsum("ayc,ax->xyc", inner_mixed, outer_part, precision=lax.Precision.HIGHEST)
    return (
        turned.reshape(part_width * FACTOR_B, full_rows.shape[1]) * (1.0 / math.sqrt(D))
    ).astype(jnp.bfloat16)


def rotate_columns(matrix):
    outer_factor, inner_factor = hadamard_pair()
    height = matrix.shape[0]
    blocks = matrix.reshape(height, FACTOR_A, FACTOR_B)
    inner_mixed = jnp.einsum(
        "mab,by->may", blocks, inner_factor.astype(jnp.bfloat16), preferred_element_type=jnp.float32
    )
    turned = jnp.einsum("may,ax->mxy", inner_mixed, outer_factor, precision=lax.Precision.HIGHEST)
    return (turned.reshape(height, D) * (1.0 / math.sqrt(D))).astype(jnp.bfloat16)


def fold_columns(block):
    spread = lax.all_to_all(block, "shard", split_axis=0, concat_axis=1, tiled=True)
    turned = rotate_columns(spread)
    return lax.all_to_all(turned, "shard", split_axis=1, concat_axis=0, tiled=True)


def rotary(vectors, positions):
    half_dim = HEAD_DIM // 2
    frequency = jnp.power(
        jnp.float32(ROPE_BASE), -jnp.arange(0, HEAD_DIM, 2, dtype=jnp.float32) / HEAD_DIM
    )
    angles = positions.astype(jnp.float32)[:, :, None] * frequency[None, None, :]
    cosine = jnp.cos(angles)[:, :, None, :]
    sine = jnp.sin(angles)[:, :, None, :]
    first, second = (vectors[..., :half_dim], vectors[..., half_dim:])
    return jnp.concatenate(
        [first * cosine - second * sine, second * cosine + first * sine], axis=-1
    )


def normalize(states, gain):
    mean_square = jnp.mean(states * states, axis=-1, keepdims=True)
    return (states * lax.rsqrt(mean_square + EPSILON) * gain.astype(jnp.float32)).astype(
        jnp.bfloat16
    )


def attend(packed, keys, values, lengths):
    rows = packed.shape[0]
    cached = keys.shape[1]
    group_size = HEADS // KV_HEADS
    positions = lengths[:, None] + jnp.arange(STEPS, dtype=jnp.int32)[None, :]
    queries = rotary(
        packed[:, :, :QDIM].astype(jnp.float32).reshape(rows, STEPS, HEADS, HEAD_DIM), positions
    ).astype(jnp.bfloat16)
    new_keys = rotary(
        packed[:, :, QDIM : QDIM + KVD]
        .astype(jnp.float32)
        .reshape(rows, STEPS, KV_HEADS, HEAD_DIM),
        positions,
    ).astype(jnp.bfloat16)
    new_values = packed[:, :, QDIM + KVD :].reshape(rows, STEPS, KV_HEADS, HEAD_DIM)
    queries = queries.reshape(rows, STEPS, KV_HEADS, group_size, HEAD_DIM)
    cached_keys = keys.reshape(rows, cached, KV_HEADS, HEAD_DIM)
    cached_values = values.reshape(rows, cached, KV_HEADS, HEAD_DIM)
    score_scale = 1.0 / math.sqrt(HEAD_DIM)
    old_scores = (
        jnp.einsum("rtkgd,rpkd->rtkgp", queries, cached_keys, preferred_element_type=jnp.float32)
        * score_scale
    )
    fresh_scores = (
        jnp.einsum("rtkgd,rskd->rtkgs", queries, new_keys, preferred_element_type=jnp.float32)
        * score_scale
    )
    live_mask = jnp.arange(cached, dtype=jnp.int32)[None, :] < lengths[:, None]
    old_scores = jnp.where(live_mask[:, None, None, None, :], old_scores, -1e30)
    causal = (
        jnp.arange(STEPS, dtype=jnp.int32)[None, :] <= jnp.arange(STEPS, dtype=jnp.int32)[:, None]
    )
    fresh_scores = jnp.where(causal[None, :, None, None, :], fresh_scores, -1e30)
    row_peak = jnp.maximum(
        jnp.max(old_scores, axis=-1, keepdims=True), jnp.max(fresh_scores, axis=-1, keepdims=True)
    )
    old_exp = jnp.exp(old_scores - row_peak)
    fresh_exp = jnp.exp(fresh_scores - row_peak)
    denominator = jnp.sum(old_exp, axis=-1, keepdims=True) + jnp.sum(
        fresh_exp, axis=-1, keepdims=True
    )
    old_weights = (old_exp / denominator).astype(jnp.bfloat16)
    fresh_weights = (fresh_exp / denominator).astype(jnp.bfloat16)
    combined = jnp.einsum(
        "rtkgp,rpkd->rtkgd", old_weights, cached_values, preferred_element_type=jnp.float32
    )
    combined = combined + jnp.einsum(
        "rtkgs,rskd->rtkgd", fresh_weights, new_values, preferred_element_type=jnp.float32
    )
    return combined.reshape(rows, STEPS, QDIM).astype(jnp.bfloat16)


def body(qkv_versions, qkv_bias, o_versions, norm_gain, hidden, cache_keys, cache_values, lengths):
    trainer_side = lax.axis_index("role") == 0
    shard_index = lax.axis_index("shard")
    rep_index = lax.axis_index("rep")
    rep_total = lax.axis_size("rep")
    own_qkv = qkv_versions[0]
    own_out = o_versions[0]
    states = hidden[0].astype(jnp.float32)
    normed = normalize(states, norm_gain[0])
    full_qkv, full_out = (
        lax.all_gather(own_qkv, "rep", axis=0, tiled=True),
        lax.all_gather(own_out, "rep", axis=0, tiled=True),
    )
    column_count = full_qkv.shape[1]
    bias_columns = lax.dynamic_slice_in_dim(
        qkv_bias[0], shard_index * column_count, column_count
    ).astype(jnp.float32)
    piece = lax.all_gather(normed, "shard", axis=0, tiled=True)
    product = jnp.dot(piece.reshape(-1, D), full_qkv, preferred_element_type=jnp.float32)
    packed_columns = (product.reshape(piece.shape[0], STEPS, column_count) + bias_columns).astype(
        jnp.bfloat16
    )
    packed = lax.all_to_all(packed_columns, "shard", split_axis=0, concat_axis=2, tiled=True)
    attended = attend(packed, cache_keys[0], cache_values[0], lengths[0])
    out_width = full_out.shape[1]
    piece = lax.all_gather(attended, "shard", axis=0, tiled=True)
    product = jnp.dot(piece.reshape(-1, QDIM), full_out, preferred_element_type=jnp.float32)
    projected_columns = product.reshape(piece.shape[0], STEPS, out_width)
    projected = lax.all_to_all(projected_columns, "shard", split_axis=0, concat_axis=2, tiled=True)
    layer_out = (states + projected).astype(jnp.bfloat16)[None]
    sent_qkv, sent_out = shifted((own_qkv, own_out), "role", 1)
    fresh_qkv = jnp.where(trainer_side, own_qkv, sent_qkv)
    fresh_out = jnp.where(trainer_side, own_out, sent_out)
    fresh_full = lax.all_gather(fresh_qkv, "rep", axis=0, tiled=True)
    new_qkv = rotate_row_part(fresh_full, rep_index, rep_total)
    new_o = fold_columns(fresh_out)
    return (layer_out, new_qkv[None], new_o[None])


def solution(mesh):
    in_specs = (
        P("role", "rep", "shard"),
        P("role", None),
        P("role", "rep", "shard"),
        P("role", None),
        P("role", ("shard", "rep"), None, None),
        P("role", ("shard", "rep"), None, None),
        P("role", ("shard", "rep"), None, None),
        P("role", ("shard", "rep")),
    )
    out_specs = (
        P("role", ("shard", "rep"), None, None),
        P("role", "rep", "shard"),
        P("role", "rep", "shard"),
    )
    return jax.shard_map(body, mesh=mesh, in_specs=in_specs, out_specs=out_specs, check_vma=False)
```

profile of v0, /device:TPU:0, one launch (start us, length us, event | category | flops | bytes accessed | tf_op | source)
XLA Modules:
  0.0 619.3 jit_solution(976459807085907566)
XLA Ops:
  13.1 7.0 %collective-permute-start = (bf16[1280,1792]{1,0:T(8,128)(2,1)}, bf16[1280,1792]{1,0:T(8,128)(2,1)}, u32[]{:S(2)}, u32[]{:S(2)}) collective-permute-start(bf16[1280,1792]{1,0:T(8,128)(2,1)} %bitcast.140), channel_id=1, source_target_pairs={{0,16},{1,17},{2,18},{3,19},{4,20},{5,21},{6,22},{7,23},{8,24},{9,... | collective-permute-start | bytes 13762568 | tf_op jit(solution)/shard_map/ppermute | solution.py:26
  20.9 48.3 %all-gather.8.cloned.1.call-done = bf16[64,4,5120]{2,0,1:T(8,128)(2,1)} async-done(((bf16[16,4,5120]{2,0,1:T(8,128)(2,1)}), bf16[64,4,5120]{2,0,1:T(8,128)(2,1)}) %all-gather.8.cloned.1.call-update) | async-done | bytes 2621456 | tf_op jit(solution)/shard_map/all_gather | solution.py:175
  69.2 117.5 %all-gather.14.cloned.1.call-done = bf16[1,5120,1792]{2,1,0:T(8,128)(2,1)} async-done(((bf16[1,1280,1792]{2,1,0:T(8,128)(2,1)}), bf16[1,5120,1792]{2,1,0:T(8,128)(2,1)}) %all-gather.14.cloned.1.call-update) | async-done | bytes 18350096 | tf_op jit(solution)/shard_map/all_gather | solution.py:168
  186.8 11.9 %fusion.16 = bf16[64,4,1792]{2,0,1:T(8,128)(2,1)S(1)} fusion(bf16[64,4,5120]{2,0,1:T(8,128)(2,1)} %all-gather.8.cloned.1.call-done, bf16[1,5120,1792]{2,1,0:T(8,128)(2,1)} %all-gather.14.cloned.1.call-done, f32[1792]{0:T(1024)S(1)} %convert_reduce_fusion), kind=kOutput, calls=%fused_computation.19 | convolution fusion | flops 4698537984 | bytes 21896192 | tf_op jit(solution)/shard_map/dot_general | solution.py:176
  200.3 4.6 all-to-all-start
  205.5 3.5 copy.124
  214.7 13.5 %all-to-all-done = bf16[64,4,1792]{2,1,0:T(4,128)(2,1)S(1)} async-done(((bf16[64,4,1792]{2,1,0:T(4,128)(2,1)}), bf16[64,4,1792]{2,1,0:T(4,128)(2,1)S(1)}, u32[]{:S(2)}, u32[]{:S(2)}) %all-to-all-start) | async-done | bytes 917536 | tf_op jit(solution)/shard_map/all_to_all | solution.py:180
  232.2 5.1 fusion.87
  249.4 4.9 broadcast_select_fusion
  256.4 4.8 collective-permute-start.1
  261.3 69.2 %collective-permute-done.1 = bf16[1280,1280]{1,0:T(8,128)(2,1)S(1)} collective-permute-done((bf16[1280,1280]{1,0:T(8,128)(2,1)S(1)}, bf16[1280,1280]{1,0:T(8,128)(2,1)S(1)}, u32[]{:S(2)}, u32[]{:S(2)}) %collective-permute-start.1) | collective-permute-done | bytes 3276832 | tf_op jit(solution)/shard_map/ppermute | solution.py:26
  332.6 4.0 all-to-all-start.2
  337.2 71.5 %all-to-all-done.2 = bf16[4,320,1280]{2,1,0:T(8,128)(2,1)S(1)} async-done(((bf16[4,320,1280]{2,1,0:T(8,128)(2,1)}), bf16[4,320,1280]{2,1,0:T(8,128)(2,1)S(1)}, u32[]{:S(2)}, u32[]{:S(2)}) %all-to-all-start.2) | async-done | bytes 3276832 | tf_op jit(solution)/shard_map/all_to_all | solution.py:80
  408.8 4.2 copy.104
  413.0 5.3 reshape.244
  420.2 5.9 fusion.12
  429.3 4.0 copy.105
  433.3 3.7 all-to-all-start.3
  437.1 72.9 %all-to-all-done.3 = bf16[320,4,1280]{2,0,1:T(8,128)(2,1)S(1)} async-done(((bf16[320,4,1280]{2,0,1:T(8,128)(2,1)}), bf16[320,4,1280]{2,0,1:T(8,128)(2,1)S(1)}, u32[]{:S(2)}, u32[]{:S(2)}) %all-to-all-start.3) | async-done | bytes 3276832 | tf_op jit(solution)/shard_map/all_to_all | solution.py:82
  510.0 8.1 %fusion.4 = f32[64,4,1280]{2,0,1:T(8,128)S(1)} fusion(bf16[64,4,5120]{2,0,1:T(8,128)(2,1)} %all-gather.10.cloned.1.call-done, bf16[1,5120,1280]{2,1,0:T(8,128)(2,1)} %all-gather.16.cloned.1.call-done), kind=kOutput, calls=%fused_computation.6 | convolution fusion | flops 3355443200 | bytes 17039360 | tf_op jit(solution)/shard_map/dot_general | solution.py:184
  520.1 4.5 all-to-all-start.1
  524.6 23.3 %convolution_bitcast_fusion = f32[40,128,1792]{2,1,0:T(8,128)} fusion(bf16[40,128,1792]{2,1,0:T(8,128)(2,1)} %bitcast.141), kind=kOutput, calls=%fused_computation.4 | convolution fusion | flops 2349400064 | bytes 55050240 | tf_op jit(solution)/shard_map/abc,by->ayc/dot_general | solution.py:57
  548.0 49.8 %multiply_convert_fusion = bf16[10,128,1792]{2,0,1:T(8,128)(2,1)S(1)} fusion(f32[40,128,1792]{2,1,0:T(8,128)} %convolution_bitcast_fusion, f32[40,40]{0,1:T(8,128)S(1)} %mul.230, s32[]{:T(128)S(6)} %select_n.88), kind=kOutput, calls=%fused_computation.5 | convolution fusion | flops 1105592320 | bytes 41295876 | tf_op jit(solution)/shard_map/ayc,ax->xyc/dot_general | solution.py:62
  597.8 3.6 copy.103
  (85 shorter events, 53.2 us)
Async XLA Ops:
  7.2 62.1 %all-gather.8.cloned.1.call-start = ((), (), s32[]{:S(2)}) async-start(), calls=%async_computation.4 | async-start | bytes 3276800 | tf_op jit(solution)/shard_map/all_gather | solution.py:175
  11.6 175.2 %all-gather.14.cloned.1.call-start = ((), (), s32[]{:S(2)}) async-start(), calls=%async_computation.7 | async-start | bytes 22937600 | tf_op jit(solution)/shard_map/all_gather | solution.py:168
  12.4 8.5 %copy-start.4 = (s32[1,16]{1,0:T(1,128)S(1)}, s32[1,16]{1,0:T(1,128)}, u32[]{:S(2)}) copy-start(s32[1,16]{1,0:T(1,128)} %param.17) | copy-start | bytes 196
  12.4 497.7 %all-gather.16.cloned.1.call-start = ((), (), s32[]{:S(2)}) async-start(), calls=%async_computation.8 | async-start | bytes 16384000 | tf_op jit(solution)/shard_map/all_gather | solution.py:169
  13.1 236.3 %collective-permute-start = (bf16[1280,1792]{1,0:T(8,128)(2,1)}, bf16[1280,1792]{1,0:T(8,128)(2,1)}, u32[]{:S(2)}, u32[]{:S(2)}) collective-permute-start(bf16[1280,1792]{1,0:T(8,128)(2,1)} %bitcast.140), channel_id=1, source_target_pairs={{0,16},{1,17},{2,18},{3,19},{4,20},{5,21},{6,22},{7,23},{8,24},{9,... | collective-permute-start | bytes 13762568 | tf_op jit(solution)/shard_map/ppermute | solution.py:26
  200.3 27.9 %all-to-all-start = ((bf16[64,4,1792]{2,1,0:T(4,128)(2,1)}), bf16[64,4,1792]{2,1,0:T(4,128)(2,1)S(1)}, u32[]{:S(2)}, u32[]{:S(2)}) async-start(bf16[64,4,1792]{2,1,0:T(4,128)(2,1)} %copy.84), calls=%async_computation | async-start | bytes 1835008 | tf_op jit(solution)/shard_map/all_to_all | solution.py:180
  204.9 305.1 %all-gather.10.cloned.1.call-start = ((), (), s32[]{:S(2)}) async-start(), calls=%async_computation.5 | async-start | bytes 3276800 | tf_op jit(solution)/shard_map/all_gather | solution.py:183
  205.5 3.5 copy-start.2
  231.8 5.5 copy-start
  243.1 2.2 copy-start.3
  249.4 275.3 %all-gather.12.cloned.1.call-start = ((), (), s32[]{:S(2)}) async-start(), calls=%async_computation.6 | async-start | bytes 22937600 | tf_op jit(solution)/shard_map/all_gather | solution.py:191
  254.3 2.1 copy-start.1
  256.4 74.1 %collective-permute-start.1 = (bf16[1280,1280]{1,0:T(8,128)(2,1)S(1)}, bf16[1280,1280]{1,0:T(8,128)(2,1)S(1)}, u32[]{:S(2)}, u32[]{:S(2)}) collective-permute-start(bf16[1280,1280]{1,0:T(8,128)(2,1)S(1)} %bitcast.144), channel_id=1, source_target_pairs={{0,16},{1,17},{2,18},{3,19},{4,20},{5,21},{6,22},{7,23},{8,24},{9,... | collective-permute-start | bytes 9830408 | tf_op jit(solution)/shard_map/ppermute | solution.py:26
  332.6 4.2 copy-start.6
  332.6 4.4 copy-start.5
  332.6 76.1 %all-to-all-start.2 = ((bf16[4,320,1280]{2,1,0:T(8,128)(2,1)}), bf16[4,320,1280]{2,1,0:T(8,128)(2,1)S(1)}, u32[]{:S(2)}, u32[]{:S(2)}) async-start(bf16[4,320,1280]{2,1,0:T(8,128)(2,1)} %bitcast.147), calls=%async_computation.2 | async-start | bytes 6553600 | tf_op jit(solution)/shard_map/all_to_all | solution.py:80
  433.3 76.7 %all-to-all-start.3 = ((bf16[320,4,1280]{2,0,1:T(8,128)(2,1)}), bf16[320,4,1280]{2,0,1:T(8,128)(2,1)S(1)}, u32[]{:S(2)}, u32[]{:S(2)}) async-start(bf16[320,4,1280]{2,0,1:T(8,128)(2,1)} %copy.105), calls=%async_computation.3 | async-start | bytes 6553600 | tf_op jit(solution)/shard_map/all_to_all | solution.py:82
  520.1 81.3 %all-to-all-start.1 = ((f32[64,4,1280]{2,1,0:T(4,128)}), f32[64,4,1280]{2,1,0:T(4,128)}, u32[]{:S(2)}, u32[]{:S(2)}) async-start(f32[64,4,1280]{2,1,0:T(4,128)} %copy.98), calls=%async_computation.1 | async-start | bytes 2621440 | tf_op jit(solution)/shard_map/all_to_all | solution.py:186
Sparse Core Ops, SparseCore 0:
  11.7 57.4 all-gather.7
  70.8 115.9 all-gather.13
  188.3 85.0 all-gather.15
  275.5 54.7 all-gather.9
  332.3 115.9 all-gather.11
where the time goes:
time: 625 us; the launch traced here: 619 us
  waiting for transfers between devices  395 us (63%)
  matrix products  112 us (18%)
  local copies, waits for them, and re-layouts  50.5 us (8%)
  starting transfers between devices  29 us (5%)
  other arithmetic  18.2 us (3%)
  between operations  14.6 us (2%)
    all_gather x1, waiting for transfers between devices, body(): lax.all_gather(own_qkv, 'rep', axis=0, tiled=True)  118 us
    all_to_all x1, waiting for transfers between devices, fold_columns(): lax.all_to_all(turned, 'shard', split_axis=1, concat_axis=0, tiled=True)  72.9 us
    all_to_all x1, waiting for transfers between devices, fold_columns(): lax.all_to_all(block, 'shard', split_axis=0, concat_axis=1, tiled=True)  71.5 us
    ppermute x2, waiting for transfers between devices, shifted(): lax.ppermute(value, axis, [(source, source + steps) for source in range(i...  69.2 us
    dot_general x1, matrix products, rotate_row_part(): jnp.einsum('ayc,ax->xyc', inner_mixed, outer_part, precision=lax.Precisio...  49.8 us
    all_gather x1, waiting for transfers between devices, body(): piece = lax.all_gather(normed, 'shard', axis=0, tiled=True)  48.3 us
    dot_general x1, matrix products, rotate_row_part(): jnp.einsum('abc,by->ayc', blocks, inner_factor.astype(jnp.bfloat16), pref...  23.3 us
    all_to_all x1, waiting for transfers between devices, body(): lax.all_to_all(packed_columns, 'shard', split_axis=0, concat_axis=2, tile...  13.5 us
  transfers between devices with their start and end apart: 11, of which 6 were waited for; matrix products, arithmetic and copies ran while one was open for 26% of the time, Pallas kernels for 0%

commit v1 on v0

--- a/solution.py
+++ b/solution.py
@@ -1,8 +1,12 @@
+import functools
 import math
 
 import jax
 import jax.numpy as jnp
+import numpy as np
 from jax import lax
+from jax.experimental import pallas as pl
+from jax.experimental.pallas import tpu as pltpu
 from jax.sharding import PartitionSpec as P
 
 FACTOR_A = 40
@@ -20,66 +24,191 @@
 ROPE_BASE = 1000000.0
 
 
-def shifted(value, axis, steps):
-    count = lax.axis_size(axis)
-    initial, last = (max(0, -steps), min(count, count - steps))
-    return lax.ppermute(value, axis, [(source, source + steps) for source in range(initial, last)])
-
-
-def hadamard_pair():
+MESH = pl.DeviceIdType.MESH
+
+
+def rotation_core():
     modulus = FACTOR_A // 2 - 1
-    residues = jnp.arange(modulus, dtype=jnp.int32)
-    squares = jnp.arange(1, modulus, dtype=jnp.int32) ** 2 % modulus
-    differ = (residues[None, :] - residues[:, None]) % modulus
-    residue_mask = jnp.any(differ[:, :, None] == squares[None, None, :], axis=2)
-    jacobs = jnp.where(differ == 0, 0.0, jnp.where(residue_mask, 1.0, -1.0)).astype(jnp.float32)
-    top_row = jnp.concatenate(
-        [jnp.zeros((1, 1), jnp.float32), jnp.ones((1, modulus), jnp.float32)], axis=1
-    )
-    lower_rows = jnp.concatenate([-jnp.ones((modulus, 1), jnp.float32), jacobs], axis=1)
-    paley_core = jnp.eye(modulus + 1, dtype=jnp.float32) + jnp.concatenate(
-        [top_row, lower_rows], axis=0
-    )
-    doubler = jnp.array([[1.0, 1.0], [1.0, -1.0]], jnp.float32)
-    outer_factor = jnp.kron(doubler, paley_core)
-    indices = jnp.arange(FACTOR_B, dtype=jnp.int32)
-    common_bits = indices[:, None] & indices[None, :]
-    parity = jnp.zeros((FACTOR_B, FACTOR_B), jnp.int32)
-    for bit_level in range(FACTOR_B.bit_length() - 1):
-        parity = parity + (common_bits >> bit_level & 1)
-    inner_factor = (1 - 2 * (parity % 2)).astype(jnp.float32)
-    return (outer_factor, inner_factor)
-
-
-def rotate_row_part(full_rows, part_index, part_total):
-    outer_factor, inner_factor = hadamard_pair()
-    blocks = full_rows.reshape(FACTOR_A, FACTOR_B, full_rows.shape[1])
-    inner_mixed = jnp.einsum(
-        "abc,by->ayc", blocks, inner_factor.astype(jnp.bfloat16), preferred_element_type=jnp.float32
-    )
-    part_width = FACTOR_A // part_total
-    outer_part = lax.dynamic_slice_in_dim(outer_factor, part_index * part_width, part_width, 1)
-    turned = jnp.einsum("ayc,ax->xyc", inner_mixed, outer_part, precision=lax.Precision.HIGHEST)
-    return (
-        turned.reshape(part_width * FACTOR_B, full_rows.shape[1]) * (1.0 / math.sqrt(D))
-    ).astype(jnp.bfloat16)
-
-
-def rotate_columns(matrix):
-    outer_factor, inner_factor = hadamard_pair()
+    squares = {k * k % modulus for k in range(1, modulus)}
+    paley = np.ones((modulus + 1, modulus + 1), np.float32)
+    paley[1:, 0] = -1.0
+    for i in range(modulus):
+        for j in range(modulus):
+            if i != j:
+                paley[i + 1, j + 1] = 1.0 if (j - i) % modulus in squares else -1.0
+    inner = np.ones((1, 1), np.float32)
+    while inner.shape[0] < FACTOR_B:
+        inner = np.kron(inner, np.array([[1, 1], [1, -1]], np.float32))
+    return np.kron(paley, inner).astype(jnp.bfloat16)
+
+
+def exchange_kernel(shards, reps, chunks, normed, own_q, own_o, n_all, q_all, rec_o, w_o,
+                    n_send, n_recv, y_send, y_recv, s_send, s_recv, f_send, f_recv,
+                    x_send, x_recv, a_send, a_recv, load, store, q_hold, n_hold, o_hold):
+    role, shard, rep = lax.axis_index("role"), lax.axis_index("shard"), lax.axis_index("rep")
+    planes = reps // 2
+    near = rep + 1 - 2 * lax.rem(rep, 2)
+    far = [lax.rem(rep + 2 * h, reps) for h in range(planes)]
+    back = [lax.rem(rep - 2 * h + reps, reps) for h in range(planes)]
+    peer = [lax.rem(shard + k, shards) for k in range(shards)]
+
+    greeted = [{"role": 1 - role}, {"rep": near}]
+    greeted += [{"rep": far[h]} for h in range(1, planes)]
+    greeted += [{"shard": peer[k]} for k in range(1, shards)]
+    barrier = pltpu.get_barrier_semaphore()
+    for device in greeted:
+        pl.semaphore_signal(barrier, inc=1, device_id=device, device_id_type=MESH)
+    pl.semaphore_wait(barrier, len(greeted))
+
+    def remote(src, dst, send, recv, device):
+        return pltpu.make_async_remote_copy(
+            src_ref=src, dst_ref=dst, send_sem=send, recv_sem=recv,
+            device_id=device, device_id_type=MESH)
+
+    raw = remote(own_o.at[1], rec_o, x_send, x_recv, {"role": 1 - role})
+
+    @pl.when(role == 0)
+    def _():
+        raw.start()
+
+    tokens = [remote(normed, n_all.at[shard], n_send.at[k], n_recv.at[k], {"shard": peer[k]})
+              for k in range(1, shards)]
+    across = [[remote(own_q.at[c], q_all.at[rep, c], y_send.at[h - 1, c], y_recv.at[h - 1, c],
+                      {"rep": far[h]}) for c in range(chunks)] for h in range(1, planes)]
+    aside = remote(own_q, q_all.at[rep], s_send, s_recv, {"rep": near})
+    onward = [[remote(q_all.at[back[h], c], q_all.at[back[h], c], f_send.at[h - 1, c],
+                      f_recv.at[h - 1, c], {"rep": near}) for c in range(chunks)]
+              for h in range(1, planes)]
+    for c in range(chunks):
+        for h in range(planes - 1):
+            across[h][c].start()
+    for copy in tokens:
+        copy.start()
+    aside.start()
+    own_in = [pltpu.make_async_copy(own_q.at[c], q_hold.at[c], load.at[c]) for c in range(chunks)]
+    own_in.append(pltpu.make_async_copy(normed, n_hold, load.at[chunks]))
+    own_out = [pltpu.make_async_copy(q_hold.at[c], q_all.at[rep, c], store.at[c])
+               for c in range(chunks)]
+    own_out.append(pltpu.make_async_copy(n_hold, n_all.at[shard], store.at[chunks]))
+    for copy in own_in:
+        copy.start()
+
+    def fold(source):
+        copies = [remote(source.at[peer[k]], w_o.at[shard], a_send.at[k], a_recv.at[k],
+                         {"shard": peer[k]}) for k in range(1, shards)]
+        return (copies, pltpu.make_async_copy(source.at[shard], o_hold, load.at[chunks + 1]),
+                pltpu.make_async_copy(o_hold, w_o.at[shard], store.at[chunks + 1]))
+
+    @pl.when(role == 0)
+    def _():
+        copies, fetch, keep = fold(own_o.at[0])
+        for copy in copies:
+            copy.start()
+        fetch.start()
+        fetch.wait()
+        keep.start()
+
+    for fetched, stored in zip(own_in, own_out):
+        fetched.wait()
+        stored.start()
+
+    for c in range(chunks):
+        for h in range(planes - 1):
+            across[h][c].wait_recv()
+            onward[h][c].start()
+        if c == min(1, chunks - 1):
+            @pl.when(role == 1)
+            def _():
+                raw.wait_recv()
+                copies, fetch, keep = fold(rec_o)
+                for copy in copies:
+                    copy.start()
+                fetch.start()
+                fetch.wait()
+                keep.start()
+
+    for copy in tokens:
+        copy.wait()
+    aside.wait()
+    for copy in own_out:
+        copy.wait()
+    copies, _, keep = fold(rec_o)
+    for copy in copies:
+        copy.wait()
+    keep.wait()
+    for c in range(chunks):
+        for h in range(planes - 1):
+            across[h][c].wait_send()
+            onward[h][c].wait()
+
+    @pl.when(role == 0)
+    def _():
+        raw.wait_send()
+
+
+def exchange(normed, own_q, own_o):
+    shards, reps = lax.axis_size("shard"), lax.axis_size("rep")
+    rows, width = normed.shape
+    depth, columns = own_q.shape
+    height, out_columns = own_o.shape
+    chunks = 5 if depth % 80 == 0 else 1
+    half = height // 2
+    part = half // shards
+    kind = normed.dtype
+    dma = pltpu.SemaphoreType.DMA
+    planes = max(reps // 2 - 1, 1)
+    n_all, q_all, _, w_o = pl.pallas_call(
+        functools.partial(exchange_kernel, shards, reps, chunks),
+        out_shape=(
+            jax.ShapeDtypeStruct((shards, rows, width), kind),
+            jax.ShapeDtypeStruct((reps, chunks, depth // chunks, columns), kind),
+            jax.ShapeDtypeStruct((shards, part, out_columns), kind),
+            jax.ShapeDtypeStruct((shards, part, out_columns), kind),
+        ),
+        in_specs=[pl.BlockSpec(memory_space=pl.ANY)] * 3,
+        out_specs=(pl.BlockSpec(memory_space=pl.ANY),) * 4,
+        scratch_shapes=[
+            dma((shards,)), dma((shards,)),
+            dma((planes, chunks)), dma((planes, chunks)),
+            dma, dma,
+            dma((planes, chunks)), dma((planes, chunks)),
+            dma, dma,
+            dma((shards,)), dma((shards,)),
+            dma((chunks + 2,)), dma((chunks + 2,)),
+            pltpu.VMEM((chunks, depth // chunks, columns), kind),
+            pltpu.VMEM((rows, width), kind),
+            pltpu.VMEM((part, out_columns), kind),
+        ],
+        compiler_params=pltpu.CompilerParams(
+            collective_id=0, has_side_effects=True, vmem_limit_bytes=16 * 1024 * 1024),
+        name="exchange",
+    )(normed, own_q.reshape(chunks, depth // chunks, columns),
+      own_o.reshape(2, shards, part, out_columns))
+    return n_all, q_all.reshape(reps * depth, columns), w_o
+
+
+def rotate_row_part(full_rows, core, part_index, part_total):
+    order = core.shape[0]
+    per_half = part_total // 2
+    sign = jnp.where(part_index < per_half, 1.0, -1.0).astype(jnp.float32)
+    top = full_rows[:order].astype(jnp.float32)
+    bottom = full_rows[order:].astype(jnp.float32)
+    mixed = (top + sign * bottom).astype(jnp.bfloat16)
+    count = order // per_half
+    part = lax.dynamic_slice_in_dim(core, lax.rem(part_index, per_half) * count, count, 0)
+    turned = jnp.dot(part, mixed, preferred_element_type=jnp.float32)
+    return (turned * (1.0 / math.sqrt(D))).astype(jnp.bfloat16)
+
+
+def rotate_columns(matrix, core):
     height = matrix.shape[0]
-    blocks = matrix.reshape(height, FACTOR_A, FACTOR_B)
-    inner_mixed = jnp.einsum(
-        "mab,by->may", blocks, inner_factor.astype(jnp.bfloat16), preferred_element_type=jnp.float32
-    )
-    turned = jnp.einsum("may,ax->mxy", inner_mixed, outer_factor, precision=lax.Precision.HIGHEST)
-    return (turned.reshape(height, D) * (1.0 / math.sqrt(D))).astype(jnp.bfloat16)
-
-
-def fold_columns(block):
-    spread = lax.all_to_all(block, "shard", split_axis=0, concat_axis=1, tiled=True)
-    turned = rotate_columns(spread)
-    return lax.all_to_all(turned, "shard", split_axis=1, concat_axis=0, tiled=True)
+    order = core.shape[0]
+    left = matrix[:, :order].astype(jnp.float32)
+    right = matrix[:, order:].astype(jnp.float32)
+    mixed = jnp.concatenate([left + right, left - right], axis=0).astype(jnp.bfloat16)
+    turned = jnp.dot(mixed, core, preferred_element_type=jnp.float32)
+    turned = (turned * (1.0 / math.sqrt(D))).astype(jnp.bfloat16)
+    return jnp.concatenate([turned[:height], turned[height:]], axis=1)
 
 
 def rotary(vectors, positions):
@@ -164,33 +293,40 @@
     own_out = o_versions[0]
     states = hidden[0].astype(jnp.float32)
     normed = normalize(states, norm_gain[0])
-    full_qkv, full_out = (
-        lax.all_gather(own_qkv, "rep", axis=0, tiled=True),
-        lax.all_gather(own_out, "rep", axis=0, tiled=True),
-    )
+    piece, full_qkv, folded = exchange(normed.reshape(-1, D), own_qkv, own_out)
+    late_out, _ = lax.optimization_barrier((own_out, piece))
+    full_out = lax.all_gather(late_out, "rep", axis=0, tiled=True)
+    core = jnp.asarray(rotation_core())
+
     column_count = full_qkv.shape[1]
     bias_columns = lax.dynamic_slice_in_dim(
         qkv_bias[0], shard_index * column_count, column_count
     ).astype(jnp.float32)
-    piece = lax.all_gather(normed, "shard", axis=0, tiled=True)
     product = jnp.dot(piece.reshape(-1, D), full_qkv, preferred_element_type=jnp.float32)
-    packed_columns = (product.reshape(piece.shape[0], STEPS, column_count) + bias_columns).astype(
+    packed_columns = (product.reshape(-1, STEPS, column_count) + bias_columns).astype(
         jnp.bfloat16
     )
+    turned_out = rotate_columns(jnp.swapaxes(folded, 0, 1).reshape(folded.shape[1], D), core)
+    turned_qkv = rotate_row_part(full_qkv, core.T, rep_index, rep_total)
     packed = lax.all_to_all(packed_columns, "shard", split_axis=0, concat_axis=2, tiled=True)
+    mine = lax.all_to_all(turned_out, "shard", split_axis=1, concat_axis=0, tiled=True)
+    sent_qkv = lax.ppermute(turned_qkv, "role", [(0, 1)])
+
+    packed, turned_qkv, _ = lax.optimization_barrier((packed, turned_qkv, turned_out))
     attended = attend(packed, cache_keys[0], cache_values[0], lengths[0])
+    attended, full_out, mine = lax.optimization_barrier((attended, full_out, mine))
+    theirs = lax.ppermute(mine, "role", [(0, 1), (1, 0)])
     out_width = full_out.shape[1]
     piece = lax.all_gather(attended, "shard", axis=0, tiled=True)
     product = jnp.dot(piece.reshape(-1, QDIM), full_out, preferred_element_type=jnp.float32)
-    projected_columns = product.reshape(piece.shape[0], STEPS, out_width)
+    projected_columns = product.reshape(piece.shape[0], STEPS, out_width).astype(jnp.bfloat16)
     projected = lax.all_to_all(projected_columns, "shard", split_axis=0, concat_axis=2, tiled=True)
-    layer_out = (states + projected).astype(jnp.bfloat16)[None]
-    sent_qkv, sent_out = shifted((own_qkv, own_out), "role", 1)
-    fresh_qkv = jnp.where(trainer_side, own_qkv, sent_qkv)
-    fresh_out = jnp.where(trainer_side, own_out, sent_out)
-    fresh_full = lax.all_gather(fresh_qkv, "rep", axis=0, tiled=True)
-    new_qkv = rotate_row_part(fresh_full, rep_index, rep_total)
-    new_o = fold_columns(fresh_out)
+    layer_out = (states + projected.astype(jnp.float32)).astype(jnp.bfloat16)[None]
+
+    new_qkv = jnp.where(trainer_side, turned_qkv, sent_qkv)
+    new_o = jnp.concatenate(
+        [jnp.where(trainer_side, mine, theirs), jnp.where(trainer_side, theirs, mine)], axis=0
+    )
     return (layer_out, new_qkv[None], new_o[None])
 
 

time: 625 us -> 352 us (0.56)
  waiting for transfers between devices: 395 us -> 77.8 us
  Pallas kernels: 0 us -> 108 us
  matrix products: 112 us -> 59.7 us
  starting transfers between devices: 29 us -> 18.1 us
  local copies, waits for them, and re-layouts: 50.5 us -> 40.4 us
  other arithmetic: 18.2 us -> 26.5 us
    all_gather x4 -> x1, waiting for transfers between devices: 166 us -> 0.01 us  [body(): full_out = lax.all_gather(late_out, 'rep', axis=0, tiled=True)]
    all_to_all x2 -> x1, waiting for transfers between devices: 144 us -> 16.7 us  [body(): lax.all_to_all(turned_out, 'shard', split_axis=1, concat_axis=0, tiled=True)]
    pallas_call x0 -> x1, Pallas kernels: none -> 108 us  [exchange(): pl.pallas_call(functools.partial(exchange_kernel, shards, reps, chunks),...]
    dot_general x4 -> x2, matrix products: 80.9 us -> 23.6 us  [the longest x1 15.8 us: rotate_row_part(): turned = jnp.dot(part, mixed, preferred_element_type=jnp.float32)]
    ppermute x2, waiting for transfers between devices: 69.2 us -> 36.9 us  [the longest x1 34.3 us: body(): sent_qkv = lax.ppermute(turned_qkv, 'role', [(0, 1)])]
    all_to_all x1, waiting for transfers between devices: 13.5 us -> 0.01 us  [body(): lax.all_to_all(packed_columns, 'shard', split_axis=0, concat_axis=2, tile...]
    all_gather x1, waiting for transfers between devices: 0.01 us -> 12.9 us  [body(): piece = lax.all_gather(attended, 'shard', axis=0, tiled=True)]
    all_to_all x1, waiting for transfers between devices: 0.01 us -> 11.3 us  [body(): lax.all_to_all(projected_columns, 'shard', split_axis=0, concat_axis=2, t...]
  transfers between devices with their start and end apart: 11 -> 7, of which waited for: 6 -> 5; matrix products, arithmetic and copies ran while one was open for 26% -> 29% of each run, Pallas kernels for 0% -> 0%
where the time goes in v1:
time: 352 us; the launch traced here: 345 us
  Pallas kernels  108 us (31%)
  waiting for transfers between devices  77.8 us (22%)
  matrix products  59.7 us (17%)
  local copies, waits for them, and re-layouts  40.4 us (11%)
  other arithmetic  26.5 us (8%)
  starting transfers between devices  18.1 us (5%)
  between operations  14.9 us (4%)
    pallas_call x1, Pallas kernels, exchange(): pl.pallas_call(functools.partial(exchange_kernel, shards, reps, chunks),...  108 us
    ppermute x1, waiting for transfers between devices, body(): sent_qkv = lax.ppermute(turned_qkv, 'role', [(0, 1)])  34.3 us
    unnamed x37, local copies, waits for them, and re-layouts  18.8 us
    all_to_all x1, waiting for transfers between devices, body(): lax.all_to_all(turned_out, 'shard', split_axis=1, concat_axis=0, tiled=True)  16.7 us
    dot_general x1, matrix products, body(): jnp.dot(piece.reshape(-1, D), full_qkv, preferred_element_type=jnp.float32)  16.1 us
    dot_general x1, matrix products, rotate_row_part(): turned = jnp.dot(part, mixed, preferred_element_type=jnp.float32)  15.8 us
    all_gather x1, waiting for transfers between devices, body(): piece = lax.all_gather(attended, 'shard', axis=0, tiled=True)  12.9 us
    all_to_all x1, waiting for transfers between devices, body(): lax.all_to_all(projected_columns, 'shard', split_axis=0, concat_axis=2, t...  11.3 us
  transfers between devices with their start and end apart: 7, of which 5 were waited for; matrix products, arithmetic and copies ran while one was open for 29% of the time, Pallas kernels for 0%

profile of v1, /device:TPU:0, one launch (start us, length us, event | category | flops | bytes accessed | tf_op | source)
XLA Modules:
  0.0 345.3 jit_solution(2206497346764321226)
XLA Ops:
  7.2 2.6 reshape.189
  13.0 2.3 copy-done.2
  15.3 107.9 %exchange.1 = (bf16[4,64,5120]{2,1,0:T(8,128)(2,1)S(1)}, bf16[4,5,256,1792]{3,2,1,0:T(8,128)(2,1)S(1)}, bf16[4,160,1280]{2,1,0:T(8,128)(2,1)}, bf16[4,160,1280]{2,1,0:T(8,128)(2,1)S(1)}) custom-call(bf16[64,5120]{1,0:T(8,128)(2,1)S(1)} %multiply_convert_fusion.normed, bf16[5,256,1792]{2,1,0:T(8,128)(2,1)S(1)} %bitcast.114, ...), custom_call_target="tpu_custom_call" | custom-call | tf_op jit(solution)/shard_map/exchange/pallas_call | solution.py:160
  123.1 6.3 %copy-done = bf16[4,5,256,1792]{3,2,1,0:T(8,128)(2,1)} copy-done((bf16[4,5,256,1792]{3,2,1,0:T(8,128)(2,1)}, bf16[4,5,256,1792]{3,2,1,0:T(8,128)(2,1)S(1)}, u32[]{:S(2)}) %copy-start) | copy-done | bytes 18350104
  133.9 2.4 dot_general.26
  137.0 16.1 %fusion.10 = bf16[64,4,1792]{2,0,1:T(8,128)(2,1)S(1)} fusion(bf16[5120,1792,1]{1,0,2:T(8,128)(2,1)} %bitcast.111, bf16[64,4,5120]{2,1,0:T(4,128)(2,1)} %dot_general.26, f32[1792]{0:T(1024)S(1)} %convert_reduce_fusion), kind=kOutput, calls=%fused_computation.18 | convolution fusion | flops 4698537984 | bytes 21896192 | tf_op jit(solution)/shard_map/dot_general | solution.py:305
  154.8 3.7 %all-to-all-start = ((bf16[64,4,1792]{2,1,0:T(4,128)(2,1)}), bf16[64,4,1792]{2,1,0:T(4,128)(2,1)S(1)}, u32[]{:S(2)}, u32[]{:S(2)}) async-start(bf16[64,4,1792]{2,1,0:T(4,128)(2,1)} %copy.49), calls=%async_computation | async-start | bytes 1835008 | tf_op jit(solution)/shard_map/all_to_all | solution.py:311
  158.4 8.2 %add_convert_fusion = bf16[2,5,256,1792]{3,2,1,0:T(8,128)(2,1)S(1)} fusion(bf16[4,5,256,1792]{3,2,1,0:T(8,128)(2,1)} %copy-done, f32[]{:T(128)S(6)} %select_n.43), kind=kLoop, calls=%fused_computation | loop fusion | flops 22937600 | bytes 27525124 | tf_op jit(solution)/shard_map/convert_element_type | solution.py:196
  166.7 15.8 %fusion.2 = bf16[1280,1792]{1,0:T(8,128)(2,1)} fusion(bf16[2560,1792]{1,0:T(8,128)(2,1)S(1)} %bitcast.119, bf16[2560,2560]{1,0:T(8,128)(2,1)} %constant.59.clone, s32[]{:T(128)S(6)} %select_n.42), kind=kOutput, calls=%fused_computation.4 | convolution fusion | flops 11748638720 | bytes 20316164 | tf_op jit(solution)/shard_map/dot_general | solution.py:199
  182.5 5.7 %collective-permute-start = (bf16[1280,1792]{1,0:T(8,128)(2,1)}, bf16[1280,1792]{1,0:T(8,128)(2,1)}, u32[]{:S(2)}, u32[]{:S(2)}) collective-permute-start(bf16[1280,1792]{1,0:T(8,128)(2,1)} %fusion.2), channel_id=1, source_target_pairs={{0,16},{1,17},{2,18},{3,19},{4,20},{5,21},{6,22},{7,23},{8,24},{9,... | collective-permute-start | bytes 13762568 | tf_op jit(solution)/shard_map/ppermute | solution.py:313
  188.8 7.7 %fusion.8 = bf16[320,2560]{1,0:T(8,128)(2,1)S(1)} fusion(bf16[2560,2560]{1,0:T(8,128)(2,1)} %constant.59.clone, bf16[160,2560]{1,0:T(8,128)(2,1)S(1)} %get-tuple-element.28, bf16[160,2560]{1,0:T(8,128)(2,1)S(1)} %get-tuple-element.27), kind=kOutput, calls=%fused_computation.14 | convolution fusion | flops 4199219200 | bytes 16384000 | tf_op jit(solution)/shard_map/dot_general | solution.py:209
  203.5 2.3 bitcast_bitcast_fusion.1
  205.8 2.4 bitcast_bitcast_fusion
  208.2 5.0 %all-to-all-start.1 = ((bf16[160,4,1280]{2,0,1:T(8,128)(2,1)}), bf16[160,4,1280]{2,0,1:T(8,128)(2,1)S(1)}, u32[]{:S(2)}, u32[]{:S(2)}) async-start(bf16[160,4,1280]{2,0,1:T(8,128)(2,1)} %bitcast.107), calls=%async_computation.1 | async-start | bytes 3276800 | tf_op jit(solution)/shard_map/all_to_all | solution.py:312
  217.6 5.1 %fusion.48 = (f32[16,4,8,5]{3,1,2,0:T(4,128)S(1)}, f32[16,4,8,5,4]{3,4,1,2,0:T(4,128)S(1)}) fusion(bf16[16,4,8,5,64]{4,3,1,2,0:T(8,128)(2,1)S(1)} %copy.57, bf16[16,4,8,5,64]{4,3,1,2,0:T(8,128)(2,1)S(1)} %copy.56, bf16[16,4,8,64]{3,1,2,0:T(4,128)(2,1)S(1)} %get-tuple-element.34, bf16[16,4,8,64]{3,1,2,0:T(4,128)(2,1)S(1)} %get-tuple-element.33, ...), kind=kOutput, calls=%fused_computation.86 | convolution fusion | flops 4222464 | bytes 837648 | tf_op jit(solution)/shard_map/rtkgd,rskd->rtkgs/dot_general | solution.py:259
  222.7 2.9 bitcast_reduce_fusion
  234.7 16.7 %all-to-all-done.1 = bf16[160,4,1280]{2,0,1:T(8,128)(2,1)S(1)} async-done(((bf16[160,4,1280]{2,0,1:T(8,128)(2,1)}), bf16[160,4,1280]{2,0,1:T(8,128)(2,1)S(1)}, u32[]{:S(2)}, u32[]{:S(2)}) %all-to-all-start.1) | async-done | bytes 1638432 | tf_op jit(solution)/shard_map/all_to_all | solution.py:312
  251.5 34.3 %collective-permute-done = bf16[1280,1792]{1,0:T(8,128)(2,1)} collective-permute-done((bf16[1280,1792]{1,0:T(8,128)(2,1)}, bf16[1280,1792]{1,0:T(8,128)(2,1)}, u32[]{:S(2)}, u32[]{:S(2)}) %collective-permute-start) | collective-permute-done | bytes 4587552 | tf_op jit(solution)/shard_map/ppermute | solution.py:313
  285.7 5.0 %select_bitcast_fusion = bf16[1,1280,1792]{2,1,0:T(8,128)(2,1)} fusion(bf16[1280,1792]{1,0:T(8,128)(2,1)} %fusion.2, bf16[1280,1792]{1,0:T(8,128)(2,1)} %collective-permute-done, pred[]{:T(512)S(6)} %eq.3), kind=kLoop, calls=%fused_computation.6 | loop fusion | flops 2293760 | bytes 13762561 | tf_op jit(solution)/shard_map/broadcast_in_dim | solution.py:330
  290.7 12.9 %all-gather.5.cloned.1.call-done = bf16[64,4,5120]{2,0,1:T(8,128)(2,1)} async-done(((bf16[16,4,5120]{2,0,1:T(8,128)(2,1)}), bf16[64,4,5120]{2,0,1:T(8,128)(2,1)}) %all-gather.5.cloned.1.call-update) | async-done | bytes 2621456 | tf_op jit(solution)/shard_map/all_gather | solution.py:320
  303.6 9.1 %fusion.13 = bf16[64,4,1280]{2,0,1:T(8,128)(2,1)S(1)} fusion(bf16[64,4,5120]{2,0,1:T(8,128)(2,1)} %all-gather.5.cloned.1.call-done, bf16[5120,1280]{1,0:T(8,128)(2,1)} %all-gather.3.cloned.1.call-done), kind=kOutput, calls=%fused_computation.19 | convolution fusion | flops 3355770880 | bytes 16384000 | tf_op jit(solution)/shard_map/dot_general | solution.py:321
  314.0 3.5 %all-to-all-start.2 = ((bf16[64,4,1280]{2,1,0:T(4,128)(2,1)}), bf16[64,4,1280]{2,1,0:T(4,128)(2,1)S(1)}, u32[]{:S(2)}, u32[]{:S(2)}) async-start(bf16[64,4,1280]{2,1,0:T(4,128)(2,1)} %copy.65), calls=%async_computation.2 | async-start | bytes 1310720 | tf_op jit(solution)/shard_map/all_to_all | solution.py:323
  317.5 2.6 collective-permute-done.1
  323.7 11.3 %all-to-all-done.2 = bf16[64,4,1280]{2,1,0:T(4,128)(2,1)S(1)} async-done(((bf16[64,4,1280]{2,1,0:T(4,128)(2,1)}), bf16[64,4,1280]{2,1,0:T(4,128)(2,1)S(1)}, u32[]{:S(2)}, u32[]{:S(2)}) %all-to-all-start.2) | async-done | bytes 655392 | tf_op jit(solution)/shard_map/all_to_all | solution.py:323
  (86 shorter events, 38.8 us)
Async XLA Ops:
  7.2 4.1 %copy-start.14 = (bf16[1,5120]{1,0:T(2,128)(2,1)S(1)}, bf16[1,5120]{1,0:T(2,128)(2,1)}, u32[]{:S(2)}) copy-start(bf16[1,5120]{1,0:T(2,128)(2,1)} %param.12) | copy-start | bytes 30724
  7.2 5.8 %copy-start.1 = (bf16[1,1280,1280]{2,1,0:T(8,128)(2,1)S(1)}, bf16[1,1280,1280]{2,1,0:T(8,128)(2,1)}, u32[]{:S(2)}) copy-start(bf16[1,1280,1280]{2,1,0:T(8,128)(2,1)} %param.11) | copy-start | bytes 9830404
  7.2 244.2 %all-gather.3.cloned.1.call-start = ((), (), s32[]{:S(2)}) async-start(), calls=%async_computation.3 | async-start | bytes 16384000 | tf_op jit(solution)/shard_map/all_gather | solution.py:298
  12.9 2.3 copy-start.2
  123.1 6.3 %copy-start = (bf16[4,5,256,1792]{3,2,1,0:T(8,128)(2,1)}, bf16[4,5,256,1792]{3,2,1,0:T(8,128)(2,1)S(1)}, u32[]{:S(2)}) copy-start(bf16[4,5,256,1792]{3,2,1,0:T(8,128)(2,1)S(1)} %get-tuple-element.13) | copy-start | bytes 55050244
  129.4 1.5 copy-start.3
  130.9 1.2 copy-start.5
  132.1 1.7 copy-start.4
  154.8 53.4 %all-to-all-start = ((bf16[64,4,1792]{2,1,0:T(4,128)(2,1)}), bf16[64,4,1792]{2,1,0:T(4,128)(2,1)S(1)}, u32[]{:S(2)}, u32[]{:S(2)}) async-start(bf16[64,4,1792]{2,1,0:T(4,128)(2,1)} %copy.49), calls=%async_computation | async-start | bytes 1835008 | tf_op jit(solution)/shard_map/all_to_all | solution.py:311
  166.7 21.5 %copy-start.6 = (bf16[4,160,1280]{2,1,0:T(8,128)(2,1)S(1)}, bf16[4,160,1280]{2,1,0:T(8,128)(2,1)}, u32[]{:S(2)}) copy-start(bf16[4,160,1280]{2,1,0:T(8,128)(2,1)} %copy-done.5) | copy-start | bytes 4915204
  182.5 5.9 %copy-start.15 = (s32[1,16]{1,0:T(1,128)S(1)}, s32[1,16]{1,0:T(1,128)}, u32[]{:S(2)}) copy-start(s32[1,16]{1,0:T(1,128)} %param.16) | copy-start | bytes 196
  182.5 103.2 %collective-permute-start = (bf16[1280,1792]{1,0:T(8,128)(2,1)}, bf16[1280,1792]{1,0:T(8,128)(2,1)}, u32[]{:S(2)}, u32[]{:S(2)}) collective-permute-start(bf16[1280,1792]{1,0:T(8,128)(2,1)} %fusion.2), channel_id=1, source_target_pairs={{0,16},{1,17},{2,18},{3,19},{4,20},{5,21},{6,22},{7,23},{8,24},{9,... | collective-permute-start | bytes 13762568 | tf_op jit(solution)/shard_map/ppermute | solution.py:313
  196.5 2.4 copy-start.9
  198.9 2.2 copy-start.10
  208.2 43.2 %all-to-all-start.1 = ((bf16[160,4,1280]{2,0,1:T(8,128)(2,1)}), bf16[160,4,1280]{2,0,1:T(8,128)(2,1)S(1)}, u32[]{:S(2)}, u32[]{:S(2)}) async-start(bf16[160,4,1280]{2,0,1:T(8,128)(2,1)} %bitcast.107), calls=%async_computation.1 | async-start | bytes 3276800 | tf_op jit(solution)/shard_map/all_to_all | solution.py:312
  213.2 90.4 %all-gather.5.cloned.1.call-start = ((), (), s32[]{:S(2)}) async-start(), calls=%async_computation.4 | async-start | bytes 3276800 | tf_op jit(solution)/shard_map/all_gather | solution.py:320
  215.4 0.8 copy-start.12
  215.4 0.8 copy-start.13
  217.6 5.1 %copy-start.7 = (bf16[16,128,8,128,1]{3,2,1,0,4:T(8,128)(2,1)S(1)}, bf16[16,128,8,128,1]{3,2,1,0,4:T(8,128)(2,1)}, u32[]{:S(2)}) copy-start(bf16[16,128,8,128,1]{3,2,1,0,4:T(8,128)(2,1)} %bitcast_bitcast_fusion.1) | copy-start | bytes 12582916
  228.4 2.2 copy-start.11
  251.4 68.7 %collective-permute-start.1 = (bf16[640,1280]{1,0:T(8,128)(2,1)S(1)}, bf16[640,1280]{1,0:T(8,128)(2,1)}, u32[]{:S(2)}, u32[]{:S(2)}) collective-permute-start(bf16[640,1280]{1,0:T(8,128)(2,1)S(1)} %bitcast.122), channel_id=1, source_target_pairs={{0,16},{16,0},{1,17},{17,1},{2,18},{18,2},{3,19},{19,3},{4,20},{20... | collective-permute-start | bytes 4915208 | tf_op jit(solution)/shard_map/ppermute | solution.py:318
  314.0 21.0 %all-to-all-start.2 = ((bf16[64,4,1280]{2,1,0:T(4,128)(2,1)}), bf16[64,4,1280]{2,1,0:T(4,128)(2,1)S(1)}, u32[]{:S(2)}, u32[]{:S(2)}) async-start(bf16[64,4,1280]{2,1,0:T(4,128)(2,1)} %copy.65), calls=%async_computation.2 | async-start | bytes 1310720 | tf_op jit(solution)/shard_map/all_to_all | solution.py:323
  335.1 1.8 copy-start.8
Sparse Core Ops, SparseCore 0:
  132.3 83.2 all-gather.2
  251.5 51.9 all-gather.4
